TPU v7x, 32 devices: a whole 2x2x4 slice. The times are simulated.
32 devices in a mesh: row: 4 (over x, core), col: 8 (over z, y).
Axes of the slice: x: 2, y: 2, z: 4, core: 2. Of those that a mesh axis runs over, the one named last changes fastest.
Arguments:
- sdf_grids: bfloat16 [16384, 4096], P(('row', 'col')), may hold values from -6 to 6
- grain_poses: float32 [12, 16384], P(None, ('row', 'col')), may hold values from -4 to 4
- surface_nodes: float32 [16384, 768], P(('row', 'col')), may hold values from -5 to 5
- send_list: int32 [4, 8, 8, 32], P('row', 'col'), may hold values from 0 to 511, as said below
- pair_first: int32 [4096], P(('row', 'col')), may hold values from 0 to 511
- pair_sdf: int32 [4096], P(('row', 'col')), may hold values from 0 to 767, as said below
- pair_pose: int32 [4096], P(('row', 'col')), may hold values from 0 to 4607, as said below
- pair_live: int32 [4096], P(('row', 'col')), may hold values from 0 to 1, as said below
- knot_cells: int32 [4096, 768], P(('row', 'col')), may hold values from 1 to 13
- offsets: float32 [4096, 768], P(('row', 'col')), may hold values from 0 to 1
Outputs:
- grain_loads: float32 [6, 16384], P(None, ('row', 'col'))
Inputs may be any that keep to these rules, and one draw needn't show every extreme that they name: `send_list`: the 8 lists of one device name distinct own grains each; list d is meant for the neighbour at offset d of the direction order; the neighbour's pairs name only slots of list d below a count from 8 to 32; on every device one of its 8 lists has count 32. `pair_sdf`: below 512: an own grain other than the first grain. From 512 on: ghost block d and slot s of an existing neighbour. `pair_pose`: names the pose of the same grain as pair_sdf: an own grain in the centre block, or the neighbour's listed grain. `pair_live`: on each device the live slots come first; their number is 128 divided by 1, 2 or 4, and some device has all slots live.
All inputs are finite; a program needn't handle non-finite values.
Results may differ from a plain program's by a relative error of at most 0.0057.
Values may be sent and summed in bfloat16 or wider, within the bound.
A program may use at most 64 MiB of HBM per device.

v0:
```python
import jax
import jax.numpy as jnp
from jax import lax
from jax.sharding import PartitionSpec as P

GRID = 16


DIRECTIONS = ((-1, -1), (-1, 0), (-1, 1), (0, -1), (0, 1), (1, -1), (1, 0), (1, 1))
STIFFNESS = 0.25
pair_block = 32


def with_halo(block, sides, width):
    for axis, dim in sides:
        count = lax.axis_size(axis)
        forward = [(i, i + 1) for i in range(count - 1)]
        backward = [(target, source) for source, target in forward]
        low = lax.ppermute(
            lax.slice_in_dim(block, block.shape[dim] - width, None, axis=dim), axis, forward
        )
        high = lax.ppermute(lax.slice_in_dim(block, 0, width, axis=dim), axis, backward)
        block = jnp.concatenate([low, block, high], axis=dim)
    return block


def passed_along(block, axis, distance):
    devices = range(lax.axis_size(axis))
    route = [(i - distance, i) for i in devices if i - distance in devices]
    return lax.ppermute(block, axis, route)


def spline_tables(knot_cell, fraction):
    complement = 1.0 - fraction
    squared = fraction * fraction
    cubed = squared * fraction
    weights = (
        complement * complement * complement / 6.0,
        (3.0 * cubed - 6.0 * squared + 4.0) / 6.0,
        (-3.0 * cubed + 3.0 * squared + 3.0 * fraction + 1.0) / 6.0,
        cubed / 6.0,
    )
    slopes = (
        -0.5 * complement * complement,
        0.5 * (3.0 * squared - 4.0 * fraction),
        0.5 * (-3.0 * squared + 2.0 * fraction + 1.0),
        0.5 * squared,
    )
    cell_ids = jnp.arange(GRID, dtype=jnp.int32)[:, None]
    shape = knot_cell.shape[:2] + (GRID,) + knot_cell.shape[2:]
    basis_rows = jnp.zeros(shape, jnp.float32)
    slope_rows = jnp.zeros(shape, jnp.float32)
    for position in range(4):
        matches = cell_ids == (knot_cell + (position - 1))[:, :, None, :]
        basis_rows = basis_rows + jnp.where(
            matches, weights[position][:, :, None, :], jnp.float32(0.0)
        )
        slope_rows = slope_rows + jnp.where(
            matches, slopes[position][:, :, None, :], jnp.float32(0.0)
        )
    return (basis_rows, slope_rows)


def pair_terms(grid_rows, knot_cell, fraction, pose_first, pose_second, node_body):
    highest = lax.Precision.HIGHEST
    batch_size = grid_rows.shape[0]
    node_count = knot_cell.shape[2]
    basis_rows, slope_rows = spline_tables(knot_cell, fraction)
    x_basis = basis_rows[:, 0].astype(jnp.bfloat16)
    x_slope = slope_rows[:, 0].astype(jnp.bfloat16)
    grid_cube = grid_rows.reshape(batch_size, GRID, GRID * GRID)
    partial_plain = jnp.einsum(
        "pam,pan->pmn", grid_cube, x_basis, preferred_element_type=jnp.float32
    ).reshape(batch_size, GRID, GRID, node_count)
    partial_slope = jnp.einsum(
        "pam,pan->pmn", grid_cube, x_slope, preferred_element_type=jnp.float32
    ).reshape(batch_size, GRID, GRID, node_count)
    basis_y = basis_rows[:, 1]
    slope_y = slope_rows[:, 1]
    section_plain = jnp.einsum("pbcn,pbn->pcn", partial_plain, basis_y, precision=highest)
    section_xslope = jnp.einsum("pbcn,pbn->pcn", partial_slope, basis_y, precision=highest)
    section_yslope = jnp.einsum("pbcn,pbn->pcn", partial_plain, slope_y, precision=highest)
    basis_z = basis_rows[:, 2]
    slope_z = slope_rows[:, 2]
    distance = jnp.einsum("pcn,pcn->pn", section_plain, basis_z, precision=highest)
    gradient = jnp.stack(
        [
            jnp.einsum("pcn,pcn->pn", section_xslope, basis_z, precision=highest),
            jnp.einsum("pcn,pcn->pn", section_yslope, basis_z, precision=highest),
            jnp.einsum("pcn,pcn->pn", section_plain, slope_z, precision=highest),
        ],
        axis=1,
    )
    penetration = STIFFNESS * jax.nn.relu(-distance)
    rotation_second = pose_second[:, 3:].reshape(batch_size, 3, 3)
    rotation_first = pose_first[:, 3:].reshape(batch_size, 3, 3)
    normal = jnp.einsum("prc,pcn->prn", rotation_second, gradient, precision=highest)
    node_force = penetration[:, None, :] * normal
    lever_arm = jnp.einsum("prc,pcn->prn", rotation_first, node_body, precision=highest)
    net_force = jnp.sum(node_force, axis=2)
    moment = jnp.sum(jnp.cross(lever_arm, node_force, axis=1), axis=2)
    separation = pose_first[:, :3] - pose_second[:, :3]
    moment_other = -(jnp.cross(separation, net_force, axis=1) + moment)
    return (
        jnp.concatenate([net_force, moment], axis=1),
        jnp.concatenate([-net_force, moment_other], axis=1),
    )


def pair_loads(
    grid_table,
    pose_table,
    grain_poses,
    surface_nodes,
    pair_first,
    pair_sdf,
    pair_pose,
    pair_live,
    knot_cells,
    offsets,
):
    pair_count = pair_first.shape[0]
    node_count = knot_cells.shape[1] // 3
    block_size = min(pair_block, pair_count)
    grid_rows = jnp.take(grid_table, pair_sdf, axis=0)
    pose_first = jnp.take(grain_poses, pair_first, axis=1).T
    pose_second = jnp.take(pose_table, pair_pose, axis=1).T
    node_body = jnp.take(surface_nodes, pair_first, axis=0).reshape(pair_count, 3, node_count)
    knot_cell = knot_cells.reshape(pair_count, 3, node_count)
    fraction = offsets.reshape(pair_count, 3, node_count)
    pieces = (grid_rows, knot_cell, fraction, pose_first, pose_second, node_body)
    blocked = tuple(
        (item.reshape((pair_count // block_size, block_size) + item.shape[1:]) for item in pieces)
    )
    on_first, on_second = lax.map(lambda group: pair_terms(*group), blocked)
    alive_mask = pair_live.astype(jnp.float32)[:, None]
    on_first = on_first.reshape(pair_count, 6) * alive_mask
    on_second = on_second.reshape(pair_count, 6) * alive_mask
    return jax.ops.segment_sum(
        jnp.concatenate([on_first, on_second], axis=0),
        jnp.concatenate([pair_first, pair_sdf], axis=0),
        num_segments=grid_table.shape[0],
    )


def sectioned_routes(blocks, move_row, move_col):
    arrived = {}
    for col_step in (-1, 1):
        chosen = [direction for direction in range(8) if DIRECTIONS[direction][1] == col_step]
        carried = move_col(jnp.stack([blocks[7 - direction] for direction in chosen]), -col_step)
        for position, direction in enumerate(chosen):
            arrived[direction] = carried[position]
    for row_step in (-1, 1):
        chosen = [direction for direction in range(8) if DIRECTIONS[direction][0] == row_step]
        stacked = jnp.stack(
            [
                arrived[direction] if DIRECTIONS[direction][1] != 0 else blocks[7 - direction]
                for direction in chosen
            ]
        )
        carried = move_row(stacked, -row_step)
        for position, direction in enumerate(chosen):
            arrived[direction] = carried[position]
    return jnp.stack([arrived[direction] for direction in range(8)])


def local(
    sdf_grids,
    grain_poses,
    surface_nodes,
    send_list,
    pair_first,
    pair_sdf,
    pair_pose,
    pair_live,
    knot_cells,
    offsets,
):
    grains = sdf_grids.shape[0]
    capacity = send_list.shape[3]
    listed = send_list.reshape(8, capacity)
    outgoing = jnp.take(sdf_grids, listed.reshape(-1), axis=0).reshape(
        8, capacity, sdf_grids.shape[1]
    )
    pose_table = with_halo(grain_poses.reshape(12, 1, 1, grains), (("row", 1), ("col", 2)), 1)
    pose_table = pose_table.reshape(12, 9 * grains)
    received = sectioned_routes(
        outgoing,
        lambda payload, offset: passed_along(payload, "row", offset),
        lambda payload, offset: passed_along(payload, "col", offset),
    )
    grid_table = jnp.concatenate(
        [sdf_grids, received.reshape(8 * capacity, sdf_grids.shape[1])], axis=0
    )
    slot_sums = pair_loads(
        grid_table,
        pose_table,
        grain_poses,
        surface_nodes,
        pair_first,
        pair_sdf,
        pair_pose,
        pair_live,
        knot_cells,
        offsets,
    )
    owned_sum = slot_sums[:grains]
    reaction = slot_sums[grains:].reshape(8, capacity, 6)
    returned = sectioned_routes(
        reaction,
        lambda payload, offset: passed_along(payload, "row", offset),
        lambda payload, offset: passed_along(payload, "col", offset),
    )
    owned_sum = owned_sum + jax.ops.segment_sum(
        returned.reshape(8 * capacity, 6), listed.reshape(-1), num_segments=grains
    )
    return owned_sum.T


def solution(mesh):
    in_specs = (
        P(("row", "col"), None),
        P(None, ("row", "col")),
        P(("row", "col"), None),
        P("row", "col", None, None),
        P(("row", "col")),
        P(("row", "col")),
        P(("row", "col")),
        P(("row", "col")),
        P(("row", "col"), None),
        P(("row", "col"), None),
    )
    out_specs = P(None, ("row", "col"))
    return jax.shard_map(local, mesh=mesh, in_specs=in_specs, out_specs=out_specs, check_vma=False)
```

profile of v0, /device:TPU:0, one launch (start us, length us, event | category | flops | bytes accessed | tf_op | source)
XLA Modules:
  0.0 177.2 jit_solution(310483181897906774)
XLA Ops:
  0.0 3.1 %collective-permute-start.4 = (f32[12,1,1,512]{3,0,2,1:T(8,128)}, f32[12,1,1,512]{3,0,2,1:T(8,128)}, u32[]{:S(2)}, u32[]{:S(2)}) collective-permute-start(f32[12,1,1,512]{3,0,2,1:T(8,128)} %bitcast.243), channel_id=1, source_target_pairs={{0,8},{8,16},{16,24},{1,9},{9,17},{17,25},{2,10},{10,18},{18,26},{... | collective-permute-start | bytes 73736 | tf_op jit(solution)/shard_map/ppermute | solution.py:19
  3.1 1.3 collective-permute-start.5
  5.9 8.0 %gather_fusion = bf16[256,4096]{1,0:T(8,128)(2,1)} fusion(bf16[512,4096]{1,0:T(8,128)(2,1)} %param.12, s32[1024]{0:T(1024)S(1)} %pad_clamp_fusion.3), kind=kCustom, calls=%fused_computation | custom fusion | bytes 4195328 | tf_op jit(solution)/shard_map/jit(_take)/gather | solution.py:182
  13.9 1.8 %broadcast_select_fusion = bf16[256,4096]{1,0:T(8,128)(2,1)S(1)} fusion(bf16[256,4096]{1,0:T(8,128)(2,1)} %gather_fusion, pred[256]{0:T(512)(128)(4,1)S(1)} %compare_and_fusion.2), kind=kLoop, calls=%fused_computation.89 | loop fusion | flops 1048576 | bytes 4194560 | tf_op jit(solution)/shard_map/jit(_take)/select_n | solution.py:182
  15.8 0.8 slice_bitcast_fusion.8
  16.6 1.0 pad_maximum_fusion.2
  17.6 5.1 %collective-permute-start = (bf16[3,32,4096]{2,1,0:T(8,128)(2,1)}, bf16[3,32,4096]{2,1,0:T(8,128)(2,1)}, u32[]{:S(2)}, u32[]{:S(2)}) collective-permute-start(bf16[3,32,4096]{2,1,0:T(8,128)(2,1)} %pad_maximum_fusion.2), channel_id=1, source_target_pairs={{0,1},{1,2},{2,3},{3,4},{4,5},{5,6},{6,7},{8,9},{9,10},{10,11},{11... | collective-permute-start | bytes 2359304 | tf_op jit(solution)/shard_map/ppermute | solution.py:30
  22.7 1.0 pad_maximum_fusion.3
  23.7 1.3 collective-permute-start.1
  26.8 0.8 gather_fusion.3
  29.5 26.6 %collective-permute-done = bf16[3,32,4096]{2,1,0:T(8,128)(2,1)} collective-permute-done((bf16[3,32,4096]{2,1,0:T(8,128)(2,1)}, bf16[3,32,4096]{2,1,0:T(8,128)(2,1)}, u32[]{:S(2)}, u32[]{:S(2)}) %collective-permute-start) | collective-permute-done | bytes 786464 | tf_op jit(solution)/shard_map/ppermute | solution.py:30
  56.1 1.2 fusion.36
  57.3 1.2 fusion.37
  58.5 1.0 pad_maximum_fusion.4
  59.5 3.7 %collective-permute-start.2 = (bf16[3,32,4096]{2,1,0:T(8,128)(2,1)}, bf16[3,32,4096]{2,1,0:T(8,128)(2,1)}, u32[]{:S(2)}, u32[]{:S(2)}) collective-permute-start(bf16[3,32,4096]{2,1,0:T(8,128)(2,1)} %pad_maximum_fusion.4), channel_id=1, source_target_pairs={{0,8},{8,16},{16,24},{1,9},{9,17},{17,25},{2,10},{10,18},{18,26},{... | collective-permute-start | bytes 2359304 | tf_op jit(solution)/shard_map/ppermute | solution.py:30
  63.2 1.0 pad_maximum_fusion.5
  64.2 1.3 collective-permute-start.3
  65.6 1.2 reshape_reshape.12
  66.9 0.8 copy.226
  67.7 1.2 reshape_reshape.13
  68.9 0.8 copy.227
  71.0 4.1 %collective-permute-start.6 = (f32[12,3,1,512]{3,0,2,1:T(8,128)S(1)}, f32[12,3,1,512]{3,0,2,1:T(8,128)S(1)}, u32[]{:S(2)}, u32[]{:S(2)}) collective-permute-start(f32[12,3,1,512]{3,0,2,1:T(8,128)S(1)} %pad_maximum_fusion.7), channel_id=1, source_target_pairs={{0,1},{1,2},{2,3},{3,4},{4,5},{5,6},{6,7},{8,9},{9,10},{10,11},{11... | collective-permute-start | bytes 221192 | tf_op jit(solution)/shard_map/ppermute | solution.py:19
  75.1 1.3 collective-permute-start.7
  77.4 4.7 %collective-permute-done.7 = f32[12,3,1,512]{3,0,2,1:T(8,128)S(1)} collective-permute-done((f32[12,3,1,512]{3,0,2,1:T(8,128)S(1)}, f32[12,3,1,512]{3,0,2,1:T(8,128)S(1)}, u32[]{:S(2)}, u32[]{:S(2)}) %collective-permute-start.7) | collective-permute-done | bytes 73760 | tf_op jit(solution)/shard_map/ppermute | solution.py:22
  82.9 2.1 %copy.224 = f32[12,3,3,512]{0,3,2,1:T(8,128)} copy(f32[12,3,3,512]{3,0,2,1:T(8,128)S(1)} %pad_maximum_fusion.6) | data formatting | bytes 442368 | tf_op jit(solution)/shard_map/concatenate | solution.py:23
  85.0 2.3 %gather_fusion.2 = f32[128,12]{1,0:T(8,128)S(1)} fusion(f32[12,4608]{0,1:T(8,128)} %bitcast.239, s32[1024]{0:T(1024)S(1)} %pad_clamp_fusion.1), kind=kCustom, calls=%fused_computation.2 | custom fusion | bytes 12800 | tf_op jit(solution)/shard_map/jit(_take)/gather | solution.py:127
  88.1 1.8 %pad_maximum_fusion.1 = bf16[8,32,4096]{2,1,0:T(8,128)(2,1)S(1)} fusion(bf16[3,32,4096]{2,1,0:T(8,128)(2,1)} %collective-permute-done.3, bf16[1,32,4096]{2,1,0:T(8,128)(2,1)S(1)} %get-tuple-element.209, bf16[1,32,4096]{2,1,0:T(8,128)(2,1)S(1)} %get-tuple-element.206, bf16[3,32,4096]{2,1,0:T(8,128)(2,1)} %collective-permute-done.2), kind=kLoop, calls=%fused_computation.88 | loop fusion | flops 3145728 | bytes 4194304 | tf_op jit(solution)/shard_map/stack | solution.py:164
  89.8 0.9 copy-done.1
  90.7 3.4 %pad_maximum_fusion = bf16[768,4096]{1,0:T(8,128)(2,1)} fusion(bf16[256,4096]{1,0:T(8,128)(2,1)S(1)} %bitcast.237, bf16[512,4096]{1,0:T(8,128)(2,1)S(1)} %copy-done.1), kind=kLoop, calls=%fused_computation.87 | loop fusion | flops 12582912 | bytes 12582912 | tf_op jit(solution)/shard_map/concatenate | solution.py:192
  94.1 6.8 %gather_fusion.1 = bf16[128,4096]{1,0:T(8,128)(2,1)} fusion(bf16[768,4096]{1,0:T(8,128)(2,1)} %pad_maximum_fusion, s32[1024]{0:T(1024)S(1)} %pad_clamp_fusion.2), kind=kCustom, calls=%fused_computation.1 | custom fusion | bytes 2097664 | tf_op jit(solution)/shard_map/jit(_take)/gather | solution.py:125
  100.9 1.4 broadcast_select_fusion.1
  102.4 52.0 %while.12 = (s32[]{:T(128)}, f32[4,32,6]{1,0,2:T(4,128)S(1)}, f32[4,32,6]{1,0,2:T(4,128)S(1)}, s32[4,32,3,256]{3,1,2,0:T(8,128)}, f32[4,32,3,256]{3,1,2,0:T(8,12...) while((s32[]{:T(128)}, f32[4,32,6]{1,0,2:T(4,128)S(1)}, ...), condition=%wide.region_3.4_spmd, body=%wide.region_0.3_spmd.sunk | while | flops 157352992 | bytes 50134664 | solution.py:135
  102.6 1.0 multiply_multiply_fusion.8
  103.6 0.9 broadcast_add_fusion.5
  104.5 1.3 select_add_fusion.3
  105.9 1.3 fusion.64
  107.2 1.3 fusion.63
  108.6 3.4 %multiply_reduce_fusion.8 = (f32[32,256,16]{1,2,0:T(8,128)S(1)}, f32[32,256,16]{1,2,0:T(8,128)S(1)}, f32[32,256,16]{1,2,0:T(8,128)S(1)}) fusion(f32[32,256,16,16]{1,3,2,0:T(8,128)S(1)} %bitcast.232, f32[32,256,16]{1,2,0:T(8,128)S(1)} %get-tuple-element.329, f32[32,256,16]{1,2,0:T(8,128)S(1)} %get-tuple-element.330, f32[32,256,16,16]{1,3,2,0:T(8,128)S(1)} %bitcast.231), kind=kLoop, calls=%fused_computation.7.clone.1 | loop fusion | flops 12189696 | bytes 19398656 | tf_op jit(solution)/shard_map/while/body/eval_jaxpr/pbcn,pbn->pcn/dot_general | solution.py:82
  115.5 1.0 multiply_multiply_fusion.8
  116.5 0.9 broadcast_add_fusion.5
  117.5 1.3 select_add_fusion.3
  118.9 1.3 fusion.64
  120.2 1.3 fusion.63
  121.5 3.4 %multiply_reduce_fusion.8 = (f32[32,256,16]{1,2,0:T(8,128)S(1)}, f32[32,256,16]{1,2,0:T(8,128)S(1)}, f32[32,256,16]{1,2,0:T(8,128)S(1)}) fusion(f32[32,256,16,16]{1,3,2,0:T(8,128)S(1)} %bitcast.232, f32[32,256,16]{1,2,0:T(8,128)S(1)} %get-tuple-element.329, f32[32,256,16]{1,2,0:T(8,128)S(1)} %get-tuple-element.330, f32[32,256,16,16]{1,3,2,0:T(8,128)S(1)} %bitcast.231), kind=kLoop, calls=%fused_computation.7.clone.1 | loop fusion | flops 12189696 | bytes 19398656 | tf_op jit(solution)/shard_map/while/body/eval_jaxpr/pbcn,pbn->pcn/dot_general | solution.py:82
  128.5 1.0 multiply_multiply_fusion.8
  129.5 0.9 broadcast_add_fusion.5
  130.4 1.3 select_add_fusion.3
  131.8 1.3 fusion.64
  133.1 1.3 fusion.63
  134.5 3.4 %multiply_reduce_fusion.8 = (f32[32,256,16]{1,2,0:T(8,128)S(1)}, f32[32,256,16]{1,2,0:T(8,128)S(1)}, f32[32,256,16]{1,2,0:T(8,128)S(1)}) fusion(f32[32,256,16,16]{1,3,2,0:T(8,128)S(1)} %bitcast.232, f32[32,256,16]{1,2,0:T(8,128)S(1)} %get-tuple-element.329, f32[32,256,16]{1,2,0:T(8,128)S(1)} %get-tuple-element.330, f32[32,256,16,16]{1,3,2,0:T(8,128)S(1)} %bitcast.231), kind=kLoop, calls=%fused_computation.7.clone.1 | loop fusion | flops 12189696 | bytes 19398656 | tf_op jit(solution)/shard_map/while/body/eval_jaxpr/pbcn,pbn->pcn/dot_general | solution.py:82
  141.5 1.0 multiply_multiply_fusion.8
  142.5 0.9 broadcast_add_fusion.5
  143.4 1.3 select_add_fusion.3
  144.8 1.3 fusion.64
  146.1 1.3 fusion.63
  147.5 3.4 %multiply_reduce_fusion.8 = (f32[32,256,16]{1,2,0:T(8,128)S(1)}, f32[32,256,16]{1,2,0:T(8,128)S(1)}, f32[32,256,16]{1,2,0:T(8,128)S(1)}) fusion(f32[32,256,16,16]{1,3,2,0:T(8,128)S(1)} %bitcast.232, f32[32,256,16]{1,2,0:T(8,128)S(1)} %get-tuple-element.329, f32[32,256,16]{1,2,0:T(8,128)S(1)} %get-tuple-element.330, f32[32,256,16,16]{1,3,2,0:T(8,128)S(1)} %bitcast.231), kind=kLoop, calls=%fused_computation.7.clone.1 | loop fusion | flops 12189696 | bytes 19398656 | tf_op jit(solution)/shard_map/while/body/eval_jaxpr/pbcn,pbn->pcn/dot_general | solution.py:82
  154.7 1.7 scatter_custom_fusion
  156.7 4.6 %collective-permute-start.8 = (f32[3,32,6]{1,2,0:T(8,128)S(1)}, f32[3,32,6]{1,2,0:T(8,128)S(1)}, u32[]{:S(2)}, u32[]{:S(2)}) collective-permute-start(f32[3,32,6]{1,2,0:T(8,128)S(1)} %pad_maximum_fusion.9), channel_id=1, source_target_pairs={{0,1},{1,2},{2,3},{3,4},{4,5},{5,6},{6,7},{8,9},{9,10},{10,11},{11... | collective-permute-start | bytes 6920 | tf_op jit(solution)/shard_map/ppermute | solution.py:30
  161.5 1.3 collective-permute-start.9
  162.9 4.1 %collective-permute-done.9 = f32[3,32,6]{1,2,0:T(8,128)S(1)} collective-permute-done((f32[3,32,6]{1,2,0:T(8,128)S(1)}, f32[3,32,6]{1,2,0:T(8,128)S(1)}, u32[]{:S(2)}, u32[]{:S(2)}) %collective-permute-start.9) | collective-permute-done | bytes 2336 | tf_op jit(solution)/shard_map/ppermute | solution.py:30
  167.1 1.3 collective-permute-start.10
  168.4 1.3 collective-permute-start.11
  169.8 4.5 %collective-permute-done.11 = f32[3,32,6]{1,2,0:T(8,128)S(1)} collective-permute-done((f32[3,32,6]{1,2,0:T(8,128)S(1)}, f32[3,32,6]{1,2,0:T(8,128)S(1)}, u32[]{:S(2)}, u32[]{:S(2)}) %collective-permute-start.11) | collective-permute-done | bytes 2336 | tf_op jit(solution)/shard_map/ppermute | solution.py:30
  174.4 2.0 %scatter_fusion = f32[512,6]{1,0:T(8,128)S(1)} fusion(f32[512,6]{1,0:T(8,128)S(1)} %slice.331, s32[256]{0:T(256)S(1)} %copy-done.7, f32[256,6]{1,0:T(8,128)S(1)} %bitcast.241), kind=kCustom, calls=%fused_computation.6 | custom fusion | flops 1536 | bytes 19456 | tf_op jit(solution)/shard_map/scatter-add | solution.py:214
  (219 shorter events, 25.4 us)
Async XLA Ops:
  0.0 26.8 %copy-start = (f32[512,768]{1,0:T(8,128)S(1)}, f32[512,768]{1,0:T(8,128)}, u32[]{:S(2)}) copy-start(f32[512,768]{1,0:T(8,128)} %param.14) | copy-start | bytes 4718596
  0.0 70.2 %collective-permute-start.4 = (f32[12,1,1,512]{3,0,2,1:T(8,128)}, f32[12,1,1,512]{3,0,2,1:T(8,128)}, u32[]{:S(2)}, u32[]{:S(2)}) collective-permute-start(f32[12,1,1,512]{3,0,2,1:T(8,128)} %bitcast.243), channel_id=1, source_target_pairs={{0,8},{8,16},{16,24},{1,9},{9,17},{17,25},{2,10},{10,18},{18,26},{... | collective-permute-start | bytes 73736 | tf_op jit(solution)/shard_map/ppermute | solution.py:19
  3.1 67.1 %collective-permute-start.5 = (f32[12,1,1,512]{3,0,2,1:T(8,128)}, f32[12,1,1,512]{3,0,2,1:T(8,128)}, u32[]{:S(2)}, u32[]{:S(2)}) collective-permute-start(f32[12,1,1,512]{3,0,2,1:T(8,128)} %bitcast.244), channel_id=1, source_target_pairs={{8,0},{16,8},{24,16},{9,1},{17,9},{25,17},{10,2},{18,10},{26,18},{... | collective-permute-start | bytes 73736 | tf_op jit(solution)/shard_map/ppermute | solution.py:22
  5.1 0.8 copy-start.6
  16.6 8.4 %copy-start.11 = (s32[128]{0:T(128)S(1)}, s32[128]{0:T(128)}, u32[]{:S(2)}) copy-start(s32[128]{0:T(128)} %param.17) | copy-start | bytes 1540
  16.6 9.4 %copy-start.13 = (s32[128]{0:T(128)S(1)}, s32[128]{0:T(128)}, u32[]{:S(2)}) copy-start(s32[128]{0:T(128)} %param.16) | copy-start | bytes 1540
  16.6 9.4 %copy-start.3 = (f32[12,512]{1,0:T(8,128)S(1)}, f32[12,512]{1,0:T(8,128)}, u32[]{:S(2)}) copy-start(f32[12,512]{1,0:T(8,128)} %param.13) | copy-start | bytes 73732
  16.6 9.6 %copy-start.15 = (s32[128]{0:T(128)S(1)}, s32[128]{0:T(128)}, u32[]{:S(2)}) copy-start(s32[128]{0:T(128)} %param.18) | copy-start | bytes 1540
  17.6 38.5 %collective-permute-start = (bf16[3,32,4096]{2,1,0:T(8,128)(2,1)}, bf16[3,32,4096]{2,1,0:T(8,128)(2,1)}, u32[]{:S(2)}, u32[]{:S(2)}) collective-permute-start(bf16[3,32,4096]{2,1,0:T(8,128)(2,1)} %pad_maximum_fusion.2), channel_id=1, source_target_pairs={{0,1},{1,2},{2,3},{3,4},{4,5},{5,6},{6,7},{8,9},{9,10},{10,11},{11... | collective-permute-start | bytes 2359304 | tf_op jit(solution)/shard_map/ppermute | solution.py:30
  23.7 33.6 %collective-permute-start.1 = (bf16[3,32,4096]{2,1,0:T(8,128)(2,1)}, bf16[3,32,4096]{2,1,0:T(8,128)(2,1)}, u32[]{:S(2)}, u32[]{:S(2)}) collective-permute-start(bf16[3,32,4096]{2,1,0:T(8,128)(2,1)} %pad_maximum_fusion.3), channel_id=1, source_target_pairs={{1,0},{2,1},{3,2},{4,3},{5,4},{6,5},{7,6},{9,8},{10,9},{11,10},{12... | collective-permute-start | bytes 2359304 | tf_op jit(solution)/shard_map/ppermute | solution.py:30
  29.4 29.0 %copy-start.2 = (bf16[1,32,4096]{2,1,0:T(8,128)(2,1)S(1)}, bf16[1,32,4096]{2,1,0:T(8,128)(2,1)}, u32[]{:S(2)}) copy-start(bf16[1,32,4096]{2,1,0:T(8,128)(2,1)} %get-tuple-element.196) | copy-start | bytes 786436
  58.4 7.0 %copy-start.9 = (s32[128]{0:T(128)S(1)}, s32[128]{0:T(128)}, u32[]{:S(2)}) copy-start(s32[128]{0:T(128)} %compare_select_fusion.4) | copy-start | bytes 1540
  58.4 7.0 %copy-start.10 = (s32[128]{0:T(128)S(1)}, s32[128]{0:T(128)}, u32[]{:S(2)}) copy-start(s32[128]{0:T(128)} %compare_select_fusion.3) | copy-start | bytes 1540
  58.5 7.1 %copy-start.17 = (pred[128]{0:T(512)(128)(4,1)S(1)}, pred[128]{0:T(512)(128)(4,1)}, u32[]{:S(2)}) copy-start(pred[128]{0:T(512)(128)(4,1)} %compare_and_fusion.3) | copy-start | bytes 388
  59.5 28.6 %collective-permute-start.2 = (bf16[3,32,4096]{2,1,0:T(8,128)(2,1)}, bf16[3,32,4096]{2,1,0:T(8,128)(2,1)}, u32[]{:S(2)}, u32[]{:S(2)}) collective-permute-start(bf16[3,32,4096]{2,1,0:T(8,128)(2,1)} %pad_maximum_fusion.4), channel_id=1, source_target_pairs={{0,8},{8,16},{16,24},{1,9},{9,17},{17,25},{2,10},{10,18},{18,26},{... | collective-permute-start | bytes 2359304 | tf_op jit(solution)/shard_map/ppermute | solution.py:30
  64.2 23.9 %collective-permute-start.3 = (bf16[3,32,4096]{2,1,0:T(8,128)(2,1)}, bf16[3,32,4096]{2,1,0:T(8,128)(2,1)}, u32[]{:S(2)}, u32[]{:S(2)}) collective-permute-start(bf16[3,32,4096]{2,1,0:T(8,128)(2,1)} %pad_maximum_fusion.5), channel_id=1, source_target_pairs={{8,0},{16,8},{24,16},{9,1},{17,9},{25,17},{10,2},{18,10},{26,18},{... | collective-permute-start | bytes 2359304 | tf_op jit(solution)/shard_map/ppermute | solution.py:30
  66.8 2.9 %copy-start.16 = (s32[128]{0:T(128)S(1)}, s32[128]{0:T(128)}, u32[]{:S(2)}) copy-start(s32[128]{0:T(128)} %param.19) | copy-start | bytes 1540
  66.8 9.6 %copy-start.12 = (s32[128]{0:T(128)S(1)}, s32[128]{0:T(128)}, u32[]{:S(2)}) copy-start(s32[128]{0:T(128)} %param.17) | copy-start | bytes 1540
  66.9 9.6 %copy-start.14 = (s32[128]{0:T(128)S(1)}, s32[128]{0:T(128)}, u32[]{:S(2)}) copy-start(s32[128]{0:T(128)} %param.16) | copy-start | bytes 1540
  71.0 6.4 %collective-permute-start.6 = (f32[12,3,1,512]{3,0,2,1:T(8,128)S(1)}, f32[12,3,1,512]{3,0,2,1:T(8,128)S(1)}, u32[]{:S(2)}, u32[]{:S(2)}) collective-permute-start(f32[12,3,1,512]{3,0,2,1:T(8,128)S(1)} %pad_maximum_fusion.7), channel_id=1, source_target_pairs={{0,1},{1,2},{2,3},{3,4},{4,5},{5,6},{6,7},{8,9},{9,10},{10,11},{11... | collective-permute-start | bytes 221192 | tf_op jit(solution)/shard_map/ppermute | solution.py:19
  75.1 7.0 %collective-permute-start.7 = (f32[12,3,1,512]{3,0,2,1:T(8,128)S(1)}, f32[12,3,1,512]{3,0,2,1:T(8,128)S(1)}, u32[]{:S(2)}, u32[]{:S(2)}) collective-permute-start(f32[12,3,1,512]{3,0,2,1:T(8,128)S(1)} %pad_maximum_fusion.7), channel_id=1, source_target_pairs={{1,0},{2,1},{3,2},{4,3},{5,4},{6,5},{7,6},{9,8},{10,9},{11,10},{12... | collective-permute-start | bytes 221192 | tf_op jit(solution)/shard_map/ppermute | solution.py:22
  88.1 2.7 %copy-start.1 = (bf16[512,4096]{1,0:T(8,128)(2,1)S(1)}, bf16[512,4096]{1,0:T(8,128)(2,1)}, u32[]{:S(2)}) copy-start(bf16[512,4096]{1,0:T(8,128)(2,1)} %param.12) | copy-start | bytes 12582916
  100.9 1.4 copy-start.4
  100.9 1.4 copy-start.5
  102.4 52.2 %copy-start.8 = (f32[128]{0:T(128)S(1)}, f32[128]{0:T(128)}, u32[]{:S(2)}) copy-start(f32[128]{0:T(128)} %convert_element_type.11) | copy-start | bytes 1540
  154.4 20.0 %copy-start.7 = (s32[256]{0:T(256)S(1)}, s32[256]{0:T(256)}, u32[]{:S(2)}) copy-start(s32[256]{0:T(256)} %copy-done.6) | copy-start | bytes 3076
  156.7 6.3 %collective-permute-start.8 = (f32[3,32,6]{1,2,0:T(8,128)S(1)}, f32[3,32,6]{1,2,0:T(8,128)S(1)}, u32[]{:S(2)}, u32[]{:S(2)}) collective-permute-start(f32[3,32,6]{1,2,0:T(8,128)S(1)} %pad_maximum_fusion.9), channel_id=1, source_target_pairs={{0,1},{1,2},{2,3},{3,4},{4,5},{5,6},{6,7},{8,9},{9,10},{10,11},{11... | collective-permute-start | bytes 6920 | tf_op jit(solution)/shard_map/ppermute | solution.py:30
  161.5 5.6 %collective-permute-start.9 = (f32[3,32,6]{1,2,0:T(8,128)S(1)}, f32[3,32,6]{1,2,0:T(8,128)S(1)}, u32[]{:S(2)}, u32[]{:S(2)}) collective-permute-start(f32[3,32,6]{1,2,0:T(8,128)S(1)} %pad_maximum_fusion.10), channel_id=1, source_target_pairs={{1,0},{2,1},{3,2},{4,3},{5,4},{6,5},{7,6},{9,8},{10,9},{11,10},{12... | collective-permute-start | bytes 6920 | tf_op jit(solution)/shard_map/ppermute | solution.py:30
  167.1 2.7 %collective-permute-start.10 = (f32[3,32,6]{1,2,0:T(8,128)S(1)}, f32[3,32,6]{1,2,0:T(8,128)S(1)}, u32[]{:S(2)}, u32[]{:S(2)}) collective-permute-start(f32[3,32,6]{1,2,0:T(8,128)S(1)} %pad_maximum_fusion.11), channel_id=1, source_target_pairs={{0,8},{8,16},{16,24},{1,9},{9,17},{17,25},{2,10},{10,18},{18,26},{... | collective-permute-start | bytes 6920 | tf_op jit(solution)/shard_map/ppermute | solution.py:30
  168.4 5.8 %collective-permute-start.11 = (f32[3,32,6]{1,2,0:T(8,128)S(1)}, f32[3,32,6]{1,2,0:T(8,128)S(1)}, u32[]{:S(2)}, u32[]{:S(2)}) collective-permute-start(f32[3,32,6]{1,2,0:T(8,128)S(1)} %pad_maximum_fusion.12), channel_id=1, source_target_pairs={{8,0},{16,8},{24,16},{9,1},{17,9},{25,17},{10,2},{18,10},{26,18},{... | collective-permute-start | bytes 6920 | tf_op jit(solution)/shard_map/ppermute | solution.py:30
where the time goes:
time: 181 us; the launch traced here: 177 us
  other arithmetic  53 us (29%)
  waiting for transfers between devices  40.4 us (22%)
  local copies, waits for them, and re-layouts  38.9 us (21%)
  starting transfers between devices  29.6 us (16%)
  matrix products  13.9 us (8%)
    ppermute x8, waiting for transfers between devices, passed_along(): return lax.ppermute(block, axis, route)  35.2 us
    ppermute x8, starting transfers between devices, passed_along(): return lax.ppermute(block, axis, route)  19.9 us
    dot_general x4, other arithmetic, pair_terms(): jnp.einsum('pbcn,pbn->pcn', partial_plain, slope_y, precision=highest)  13.4 us
    gather x1, local copies, waits for them, and re-layouts, local(): jnp.take(sdf_grids, listed.reshape(-1), axis=0)  7.96 us
    ppermute x2, starting transfers between devices, with_halo(): lax.ppermute(lax.slice_in_dim(block, block.shape[dim] - width, None, axis...  7.18 us
    gather x1, local copies, waits for them, and re-layouts, pair_loads(): grid_rows = jnp.take(grid_table, pair_sdf, axis=0)  6.79 us
    add x4, other arithmetic, spline_tables(): slope_rows + jnp.where(matches, slopes[position][:, :, None, :], jnp.floa...  5.19 us
    dot_general x4, matrix products, pair_terms(): jnp.einsum('pam,pan->pmn', grid_cube, x_slope, preferred_element_type=jnp...  5.17 us
  transfers between devices with their start and end apart: 12, of which 5 were waited for; matrix products, arithmetic and copies ran while one was open for 20% of the time, Pallas kernels for 0%

commit v1 on v0

v1 whole, which is shorter than its diff:
```python
import functools

import jax
import jax.numpy as jnp
from jax import lax
from jax.experimental import pallas as pl
from jax.experimental.pallas import tpu as pltpu
from jax.sharding import PartitionSpec as P

GRID = 16
DIRECTIONS = ((-1, -1), (-1, 0), (-1, 1), (0, -1), (0, 1), (1, -1), (1, 0), (1, 1))
STIFFNESS = 0.25
CHUNKS = 4
MESH = pl.DeviceIdType.MESH
HIGHEST = lax.Precision.HIGHEST
F32 = jnp.float32
BF16 = jnp.bfloat16


def spline(knot, frac, rows):
    cell = lax.broadcasted_iota(jnp.int32, (rows, knot.shape[1]), 0).astype(F32)
    t = (knot - cell) + frac
    s = jnp.abs(t)
    p = jnp.maximum(2.0 - s, 0.0)
    q = jnp.maximum(1.0 - s, 0.0)
    p2 = p * p
    q2 = q * q
    basis = (p2 * p) * (1.0 / 6.0) - (q2 * q) * (4.0 / 6.0)
    down = 2.0 * q2 - 0.5 * p2
    slope = jnp.where(t < 0.0, -down, down)
    return basis, slope


def kernel(
    n_row, n_col, stored,
    grids, poses, nodes, lists, rows, knots, offsets,
    out,
    send_buf, ghost, pose_out, pose_in, react, ret, cube, weights, fields, lever,
    send_sem, recv_sem, psend_sem, precv_sem, rsend_sem, rrecv_sem,
):
    r = lax.axis_index("row")
    c = lax.axis_index("col")
    grains = grids.shape[0]
    capacity = lists.shape[1]
    pairs = knots.shape[0]
    count = knots.shape[1] // 3
    plane = GRID * GRID
    slots = 8 * capacity
    width = grids.shape[1] // CHUNKS

    def there(d):
        dr, dc = DIRECTIONS[d]
        rr, cc = r + dr, c + dc
        ok = (rr >= 0) & (rr < n_row) & (cc >= 0) & (cc < n_col)
        return ok, (rr, cc)

    peers = sum(there(d)[0].astype(jnp.int32) for d in range(8))
    barrier = pltpu.get_barrier_semaphore()
    for d in range(8):
        ok, place = there(d)

        @pl.when(ok)
        def _():
            pl.semaphore_signal(barrier, inc=1, device_id=place, device_id_type=MESH)

        @pl.when(jnp.logical_not(ok))
        def _():
            ghost[d * capacity:(d + 1) * capacity, :] = jnp.zeros((capacity, grids.shape[1]), BF16)
            pose_in[d] = jnp.zeros(pose_in.shape[1:], F32)
            ret[d] = jnp.zeros(ret.shape[1:], F32)

    columns = rows[...].astype(F32).T
    send_col = columns[:, 0:1]
    first_col = columns[:pairs, 1:2]
    sdf_col = columns[:pairs, 2:3]
    first_row = rows[1:2, :pairs]
    sdf_row = rows[2:3, :pairs]
    live_row = rows[3:4, :pairs].astype(F32)

    lane_grains = lax.broadcasted_iota(jnp.int32, (1, grains), 1).astype(F32)
    oh_send = jnp.where(send_col == lane_grains, 1.0, 0.0).astype(BF16)

    pose_out[...] = jnp.zeros(pose_out.shape, F32)
    sub_grains = lax.broadcasted_iota(jnp.int32, (grains, 1), 0)
    for d in range(8):
        picked = jnp.where(lists[d:d + 1, :] == sub_grains, 1.0, 0.0)
        pose_out[d, 0:12, 0:capacity] = jnp.dot(
            poses[...], picked, preferred_element_type=F32, precision=HIGHEST)

    def pose_copy(d):
        return pltpu.make_async_remote_copy(
            src_ref=pose_out.at[d], dst_ref=pose_in.at[7 - d],
            send_sem=psend_sem.at[d], recv_sem=precv_sem.at[7 - d],
            device_id=there(d)[1], device_id_type=MESH)

    def grid_copy(d, k):
        return pltpu.make_async_remote_copy(
            src_ref=send_buf.at[pl.ds(d * capacity, capacity), pl.ds(k * width, width)],
            dst_ref=ghost.at[pl.ds((7 - d) * capacity, capacity), pl.ds(k * width, width)],
            send_sem=send_sem.at[d, k], recv_sem=recv_sem.at[7 - d, k],
            device_id=there(d)[1], device_id_type=MESH)

    def react_copy(d):
        return pltpu.make_async_remote_copy(
            src_ref=react.at[d], dst_ref=ret.at[7 - d],
            send_sem=rsend_sem.at[d], recv_sem=rrecv_sem.at[7 - d],
            device_id=there(d)[1], device_id_type=MESH)

    order = (0, 2, 5, 7, 3, 4, 1, 6)
    for k in range(CHUNKS):
        def gather(j, carry, k=k):
            at = pl.ds(pl.multiple_of(k * width + j * plane, plane), plane)
            send_buf[:, at] = jnp.dot(
                oh_send, grids[:, at], preferred_element_type=F32).astype(BF16)
            return carry

        lax.fori_loop(0, width // plane, gather, 0)
        if k == 0:
            pl.semaphore_wait(barrier, peers)
        for d in order:
            @pl.when(there(d)[0])
            def _():
                grid_copy(d, k).start()
    for d in range(8):
        @pl.when(there(d)[0])
        def _():
            pose_copy(d).start()

    oh_own = jnp.where(sdf_col == lane_grains, 1.0, 0.0).astype(BF16)
    oh_first = jnp.where(first_col == lane_grains, 1.0, 0.0).astype(BF16)

    def own_cube(a, carry):
        at = pl.ds(pl.multiple_of(a * plane, plane), plane)
        found = jnp.dot(oh_own, grids[:, at], preferred_element_type=F32)
        for h in range(plane // 128):
            cube[h, pl.ds(a, pairs, stride=GRID), :] = found[:, h * 128:(h + 1) * 128]
        return carry

    lax.fori_loop(0, GRID, own_cube, 0)

    body = nodes[...]
    high = body.astype(BF16)
    low = (body - high.astype(F32)).astype(BF16)
    lever[...] = (jnp.dot(oh_first, high, preferred_element_type=F32)
                  + jnp.dot(oh_first, low, preferred_element_type=F32))

    def pair_weights(p, slot):
        knot = knots[pl.ds(p, 1), :].astype(F32)
        frac = offsets[pl.ds(p, 1), :]
        by, sy = spline(knot[:, count:2 * count], frac[:, count:2 * count], GRID)
        bz, sz = spline(knot[:, 2 * count:], frac[:, 2 * count:], GRID)
        for b in range(GRID):
            y = by[b:b + 1, :]
            weights[slot, b * GRID:(b + 1) * GRID, 0:count] = (y * bz).astype(BF16)
            weights[slot, b * GRID:(b + 1) * GRID, count:2 * count] = (
                sy[b:b + 1, :] * bz).astype(BF16)
            weights[slot, b * GRID:(b + 1) * GRID, 2 * count:] = (y * sz).astype(BF16)

    def build(p, carry):
        pair_weights(p, p)
        return carry

    lax.fori_loop(0, stored, build, 0)

    for d in range(8):
        @pl.when(there(d)[0])
        def _():
            pose_copy(d).wait_send()
            for k in range(CHUNKS):
                grid_copy(d, k).wait_send()

        back = 7 - d

        @pl.when(there(d)[0])
        def _():
            pltpu.make_async_remote_copy(
                src_ref=pose_out.at[back], dst_ref=pose_in.at[d],
                send_sem=psend_sem.at[back], recv_sem=precv_sem.at[d],
                device_id=there(d)[1], device_id_type=MESH).wait_recv()
            for k in range(CHUNKS):
                pltpu.make_async_remote_copy(
                    src_ref=send_buf.at[pl.ds(back * capacity, capacity), pl.ds(k * width, width)],
                    dst_ref=ghost.at[pl.ds(d * capacity, capacity), pl.ds(k * width, width)],
                    send_sem=send_sem.at[back, k], recv_sem=recv_sem.at[d, k],
                    device_id=there(d)[1], device_id_type=MESH).wait_recv()

    lane_slots = lax.broadcasted_iota(jnp.int32, (1, slots), 1).astype(F32)
    oh_ghost = jnp.where(sdf_col - float(grains) == lane_slots, 1.0, 0.0).astype(BF16)

    def ghost_cube(a, carry):
        at = pl.ds(pl.multiple_of(a * plane, plane), plane)
        found = jnp.dot(oh_ghost, ghost[:, at], preferred_element_type=F32)
        for h in range(plane // 128):
            cube[h, pl.ds(a, pairs, stride=GRID), :] += found[:, h * 128:(h + 1) * 128]
        return carry

    lax.fori_loop(0, GRID, ghost_cube, 0)

    def pair_fields(p, slot):
        knot = knots[pl.ds(p, 1), :].astype(F32)
        frac = offsets[pl.ds(p, 1), :]
        bx, sx = spline(knot[:, :count], frac[:, :count], GRID)
        bx = bx.astype(BF16).astype(F32)
        sx = sx.astype(BF16).astype(F32)
        at = pl.ds(pl.multiple_of(p * GRID, GRID), GRID)
        g = jnp.concatenate([cube[0, at, :], cube[1, at, :]], axis=1).astype(BF16)
        s = jnp.dot(g, weights[slot], preferred_element_type=F32)
        plain = s[:, :count]
        fields[0, pl.ds(p, 1), :] = jnp.sum(plain * bx, axis=0, keepdims=True)
        fields[1, pl.ds(p, 1), :] = jnp.sum(plain * sx, axis=0, keepdims=True)
        fields[2, pl.ds(p, 1), :] = jnp.sum(s[:, count:2 * count] * bx, axis=0, keepdims=True)
        fields[3, pl.ds(p, 1), :] = jnp.sum(s[:, 2 * count:] * bx, axis=0, keepdims=True)

    def contract(i, carry):
        for u in range(4):
            pair_fields(i * 4 + u, i * 4 + u)
        return carry

    lax.fori_loop(0, stored // 4, contract, 0)

    def late(p, carry):
        pair_weights(p, p - stored)
        pair_fields(p, p - stored)
        return carry

    if stored < pairs:
        lax.fori_loop(stored, pairs, late, 0)

    push = STIFFNESS * jnp.maximum(-fields[0], 0.0)
    lane = lax.broadcasted_iota(jnp.int32, (pairs, 128), 1)
    gathered = jnp.zeros((pairs, 128), F32)
    for k in range(3):
        g = push * fields[1 + k]
        gathered = jnp.where(lane == k, jnp.sum(g, axis=1, keepdims=True), gathered)
        for i in range(3):
            moved = jnp.sum(g * lever[:, i * count:(i + 1) * count], axis=1, keepdims=True)
            gathered = jnp.where(lane == 3 + 3 * i + k, moved, gathered)
    sums = gathered.T

    own_first = jnp.where(first_row == sub_grains, 1.0, 0.0)
    own_second = jnp.where(sdf_row == sub_grains, 1.0, 0.0)
    pose1 = jnp.dot(poses[...], own_first, preferred_element_type=F32, precision=HIGHEST)
    pose2 = jnp.dot(poses[...], own_second, preferred_element_type=F32, precision=HIGHEST)
    sub_cap = lax.broadcasted_iota(jnp.int32, (capacity, 1), 0)
    for d in range(8):
        picked = jnp.where(sdf_row - (grains + d * capacity) == sub_cap, 1.0, 0.0)
        pose2 = pose2 + jnp.dot(
            pose_in[d, 0:12, 0:capacity], picked, preferred_element_type=F32, precision=HIGHEST)

    def rot(pose, i, j):
        k = 3 + 3 * i + j
        return pose[k:k + 1, :]

    total = [sums[k:k + 1, :] for k in range(3)]
    force = [sum(rot(pose2, i, j) * total[j] for j in range(3)) for i in range(3)]
    half = [[sum(sums[3 + 3 * i + j:4 + 3 * i + j, :] * rot(pose2, s, j) for j in range(3))
             for s in range(3)] for i in range(3)]
    full = [[sum(rot(pose1, q, i) * half[i][s] for i in range(3)) for s in range(3)]
            for q in range(3)]
    moment = [full[1][2] - full[2][1], full[2][0] - full[0][2], full[0][1] - full[1][0]]
    apart = [pose1[k:k + 1, :] - pose2[k:k + 1, :] for k in range(3)]
    other = [-(apart[1] * force[2] - apart[2] * force[1] + moment[0]),
             -(apart[2] * force[0] - apart[0] * force[2] + moment[1]),
             -(apart[0] * force[1] - apart[1] * force[0] + moment[2])]
    blank = jnp.zeros((2, pairs), F32)
    on_first = jnp.concatenate(force + moment + [blank], axis=0) * live_row
    on_second = jnp.concatenate([-f for f in force] + other + [blank], axis=0) * live_row

    lane_ret = lax.broadcasted_iota(jnp.int32, (1, react.shape[2]), 1).astype(F32)
    for d in range(8):
        picked = jnp.where(sdf_col - float(grains + d * capacity) == lane_ret, 1.0, 0.0)
        react[d] = jnp.dot(on_second, picked, preferred_element_type=F32, precision=HIGHEST)

        @pl.when(there(d)[0])
        def _():
            react_copy(d).start()

    loads = (jnp.dot(on_first, oh_first.astype(F32), preferred_element_type=F32, precision=HIGHEST)
             + jnp.dot(on_second, oh_own.astype(F32), preferred_element_type=F32, precision=HIGHEST))
    for d in range(8):
        back = 7 - d

        @pl.when(there(d)[0])
        def _():
            react_copy(d).wait_send()
            pltpu.make_async_remote_copy(
                src_ref=react.at[back], dst_ref=ret.at[d],
                send_sem=rsend_sem.at[back], recv_sem=rrecv_sem.at[d],
                device_id=there(d)[1], device_id_type=MESH).wait_recv()

        picked = jnp.where(send_col[d * capacity:(d + 1) * capacity, :] == lane_grains, 1.0, 0.0)
        loads = loads + jnp.dot(
            ret[d][:, 0:capacity], picked, preferred_element_type=F32, precision=HIGHEST)
    out[...] = loads[0:6, :]


def local(
    n_row, n_col,
    sdf_grids, grain_poses, surface_nodes, send_list,
    pair_first, pair_sdf, pair_pose, pair_live, knot_cells, offsets,
):
    grains, cells = sdf_grids.shape
    capacity = send_list.shape[3]
    pairs = pair_first.shape[0]
    slots = 8 * capacity
    count = knot_cells.shape[1] // 3
    stored = min(pairs, 96)
    lists = send_list.reshape(8, capacity)
    span = max(slots, pairs)
    rows = jnp.stack([
        jnp.pad(v, (0, span - v.shape[0]))
        for v in (lists.reshape(-1), pair_first, pair_sdf, pair_live)
    ] + [jnp.zeros((span,), jnp.int32)] * 4)
    vmem = pl.BlockSpec(memory_space=pltpu.VMEM)
    return pl.pallas_call(
        functools.partial(kernel, n_row, n_col, stored),
        out_shape=jax.ShapeDtypeStruct((6, grains), F32),
        in_specs=[vmem] * 7,
        out_specs=vmem,
        scratch_shapes=[
            pltpu.VMEM((slots, cells), BF16),
            pltpu.VMEM((slots, cells), BF16),
            pltpu.VMEM((8, 16, 128), F32),
            pltpu.VMEM((8, 16, 128), F32),
            pltpu.VMEM((8, 8, 128), F32),
            pltpu.VMEM((8, 8, 128), F32),
            pltpu.VMEM((GRID * GRID // 128, pairs * GRID, 128), F32),
            pltpu.VMEM((stored, GRID * GRID, 3 * count), BF16),
            pltpu.VMEM((4, pairs, count), F32),
            pltpu.VMEM((pairs, 3 * count), F32),
            pltpu.SemaphoreType.DMA((8, CHUNKS)),
            pltpu.SemaphoreType.DMA((8, CHUNKS)),
            pltpu.SemaphoreType.DMA((8,)),
            pltpu.SemaphoreType.DMA((8,)),
            pltpu.SemaphoreType.DMA((8,)),
            pltpu.SemaphoreType.DMA((8,)),
        ],
        compiler_params=pltpu.CompilerParams(
            collective_id=0, has_side_effects=True, vmem_limit_bytes=60 * 2**20),
    )(sdf_grids, grain_poses, surface_nodes, lists, rows, knot_cells, offsets)


def solution(mesh):
    in_specs = (
        P(("row", "col"), None),
        P(None, ("row", "col")),
        P(("row", "col"), None),
        P("row", "col", None, None),
        P(("row", "col")),
        P(("row", "col")),
        P(("row", "col")),
        P(("row", "col")),
        P(("row", "col"), None),
        P(("row", "col"), None),
    )
    out_specs = P(None, ("row", "col"))
    body = functools.partial(local, mesh.shape["row"], mesh.shape["col"])
    return jax.shard_map(body, mesh=mesh, in_specs=in_specs, out_specs=out_specs, check_vma=False)
```

time: 181 us -> 66.9 us (0.37); the launches traced: 177 us -> 66.5 us
  Pallas kernels: 0 us -> 61.8 us
  other arithmetic: 53 us -> 0 us
  waiting for transfers between devices: 40.4 us -> 0 us
  local copies, waits for them, and re-layouts: 38.9 us -> 4.68 us
  starting transfers between devices: 29.6 us -> 0 us
  matrix products: 13.9 us -> 0 us
    pallas_call x0 -> x1, Pallas kernels: none -> 61.8 us  [local(): pl.pallas_call(functools.partial(kernel, n_row, n_col, stored), out_shape...]
    ppermute x12 -> x0, waiting for transfers between devices: 40.4 us -> none  [the longest x8 35.2 us: passed_along(): return lax.ppermute(block, axis, route)]
    ppermute x12 -> x0, starting transfers between devices: 29.6 us -> none  [the longest x8 19.9 us: passed_along(): return lax.ppermute(block, axis, route)]
    gather x6 -> x0, local copies, waits for them, and re-layouts: 18.7 us -> none  [the longest x1 7.96 us: local(): jnp.take(sdf_grids, listed.reshape(-1), axis=0)]
    dot_general x8 -> x0, other arithmetic: 15.7 us -> none  [the longest x4 13.4 us: pair_terms(): jnp.einsum('pbcn,pbn->pcn', partial_plain, slope_y, precision=highest)]
    dot_general x16 -> x0, matrix products: 13.9 us -> none  [the longest x4 5.17 us: pair_terms(): jnp.einsum('pam,pan->pmn', grid_cube, x_slope, preferred_element_type=jnp...]
    add x12 -> x0, other arithmetic: 8.9 us -> none  [the longest x4 5.19 us: spline_tables(): slope_rows + jnp.where(matches, slopes[position][:, :, None, :], jnp.floa...]
    select_n x9 -> x0, other arithmetic: 5.92 us -> none  [the longest x2 1.92 us: pair_loads(): grid_rows = jnp.take(grid_table, pair_sdf, axis=0)]
  transfers between devices with their start and end apart: 12 -> 0, of which waited for: 5 -> 0; matrix products, arithmetic and copies ran while one was open for 20% -> 0% of each run, Pallas kernels for 0% -> 0%
where the time goes in v1:
time: 66.9 us; the launch traced here: 66.5 us
  Pallas kernels  61.8 us (92%)
  local copies, waits for them, and re-layouts  4.68 us (7%)
    pallas_call x1, Pallas kernels, local(): pl.pallas_call(functools.partial(kernel, n_row, n_col, stored), out_shape...  61.8 us
    pad x3, local copies, waits for them, and re-layouts, local(): jnp.pad(v, (0, span - v.shape[0]))  1.97 us
    another operation x3, local copies, waits for them, and re-layouts, local(): jnp.stack([jnp.pad(v, (0, span - v.shape[0])) for v in (lists.reshape(-1)...  1.38 us

profile of v1, /device:TPU:0, one launch (start us, length us, event | category | flops | bytes accessed | tf_op | source)
XLA Modules:
  0.0 66.5 jit_solution(6570777875898712997)
XLA Ops:
  0.0 0.7 pad.10
  0.7 0.7 pad.11
  1.3 0.7 pad.12
  2.0 0.8 %stack.18 = s32[1,256]{1,0:T(1,128)S(1)} reshape(s32[1,1,8,32]{3,2,1,0:T(8,128)} %param.13) | data formatting | bytes 2048 | tf_op jit(solution)/shard_map/stack | solution.py:310
  2.7 0.6 stack.23.rows
  3.4 61.8 %shard_map.91 = f32[6,512]{1,0:T(8,128)} custom-call(bf16[512,4096]{1,0:T(8,128)(2,1)} %grids.1, f32[12,512]{1,0:T(8,128)} %poses.1, f32[512,768]{1,0:T(8,128)} %nodes.1, s32[8,32]{1,0:T(8,128)} %bitcast.6, s32[8,256]{1,0:T(8,128)} %stack.23.rows, s32[128,768]{1,0:T(8,128)} %knots.1, f32[128,768]{1,0:T(8,128)} %offsets.1), custom_call_target="tpu_custom_call" | custom-call | tf_op jit(solution)/shard_map/pallas_call | solution.py:315
  65.1 1.3 %copy.11 = f32[6,512]{1,0:T(8,128)} copy(f32[6,512]{1,0:T(8,128)} %shard_map.91) | data formatting | bytes 24576
  (1 shorter events, 0.0 us)

commit v2 on v1

--- a/solution.py
+++ b/solution.py
@@ -33,7 +33,7 @@
 
 def kernel(
     n_row, n_col, stored,
-    grids, poses, nodes, lists, rows, knots, offsets,
+    grids, poses, nodes, lists, first, second, live, knots, offsets,
     out,
     send_buf, ghost, pose_out, pose_in, react, ret, cube, weights, fields, lever,
     send_sem, recv_sem, psend_sem, precv_sem, rsend_sem, rrecv_sem,
@@ -69,13 +69,16 @@
             pose_in[d] = jnp.zeros(pose_in.shape[1:], F32)
             ret[d] = jnp.zeros(ret.shape[1:], F32)
 
-    columns = rows[...].astype(F32).T
-    send_col = columns[:, 0:1]
-    first_col = columns[:pairs, 1:2]
-    sdf_col = columns[:pairs, 2:3]
-    first_row = rows[1:2, :pairs]
-    sdf_row = rows[2:3, :pairs]
-    live_row = rows[3:4, :pairs].astype(F32)
+    first_row = first[...]
+    sdf_row = second[...]
+    live_row = live[...].astype(F32)
+    stacked = jnp.concatenate(
+        [first_row.astype(F32), sdf_row.astype(F32), jnp.zeros((6, pairs), F32)], axis=0).T
+    first_col = stacked[:, 0:1]
+    sdf_col = stacked[:, 1:2]
+    spare = jnp.zeros((8, -capacity % 128), F32)
+    turned = jnp.concatenate([lists[...].astype(F32), spare], axis=1).T
+    send_col = jnp.concatenate([turned[:capacity, d:d + 1] for d in range(8)], axis=0)
 
     lane_grains = lax.broadcasted_iota(jnp.int32, (1, grains), 1).astype(F32)
     oh_send = jnp.where(send_col == lane_grains, 1.0, 0.0).astype(BF16)
@@ -114,7 +117,7 @@
                 oh_send, grids[:, at], preferred_element_type=F32).astype(BF16)
             return carry
 
-        lax.fori_loop(0, width // plane, gather, 0)
+        lax.fori_loop(0, width // plane, gather, 0, unroll=True)
         if k == 0:
             pl.semaphore_wait(barrier, peers)
         for d in order:
@@ -133,10 +136,10 @@
         at = pl.ds(pl.multiple_of(a * plane, plane), plane)
         found = jnp.dot(oh_own, grids[:, at], preferred_element_type=F32)
         for h in range(plane // 128):
-            cube[h, pl.ds(a, pairs, stride=GRID), :] = found[:, h * 128:(h + 1) * 128]
-        return carry
-
-    lax.fori_loop(0, GRID, own_cube, 0)
+            cube[h, pl.ds(pl.multiple_of(a * pairs, pairs), pairs), :] = found[:, h * 128:(h + 1) * 128]
+        return carry
+
+    lax.fori_loop(0, GRID, own_cube, 0, unroll=4)
 
     body = nodes[...]
     high = body.astype(BF16)
@@ -191,10 +194,10 @@
         at = pl.ds(pl.multiple_of(a * plane, plane), plane)
         found = jnp.dot(oh_ghost, ghost[:, at], preferred_element_type=F32)
         for h in range(plane // 128):
-            cube[h, pl.ds(a, pairs, stride=GRID), :] += found[:, h * 128:(h + 1) * 128]
-        return carry
-
-    lax.fori_loop(0, GRID, ghost_cube, 0)
+            cube[h, pl.ds(pl.multiple_of(a * pairs, pairs), pairs), :] += found[:, h * 128:(h + 1) * 128]
+        return carry
+
+    lax.fori_loop(0, GRID, ghost_cube, 0, unroll=4)
 
     def pair_fields(p, slot):
         knot = knots[pl.ds(p, 1), :].astype(F32)
@@ -202,7 +205,7 @@
         bx, sx = spline(knot[:, :count], frac[:, :count], GRID)
         bx = bx.astype(BF16).astype(F32)
         sx = sx.astype(BF16).astype(F32)
-        at = pl.ds(pl.multiple_of(p * GRID, GRID), GRID)
+        at = pl.ds(p, GRID, stride=pairs)
         g = jnp.concatenate([cube[0, at, :], cube[1, at, :]], axis=1).astype(BF16)
         s = jnp.dot(g, weights[slot], preferred_element_type=F32)
         plain = s[:, :count]
@@ -212,19 +215,21 @@
         fields[3, pl.ds(p, 1), :] = jnp.sum(s[:, 2 * count:] * bx, axis=0, keepdims=True)
 
     def contract(i, carry):
+        for u in range(8):
+            pair_fields(i * 8 + u, i * 8 + u)
+        return carry
+
+    lax.fori_loop(0, stored // 8, contract, 0)
+
+    def late(i, carry):
         for u in range(4):
-            pair_fields(i * 4 + u, i * 4 + u)
-        return carry
-
-    lax.fori_loop(0, stored // 4, contract, 0)
-
-    def late(p, carry):
-        pair_weights(p, p - stored)
-        pair_fields(p, p - stored)
+            pair_weights(stored + i * 4 + u, i * 4 + u)
+        for u in range(4):
+            pair_fields(stored + i * 4 + u, i * 4 + u)
         return carry
 
     if stored < pairs:
-        lax.fori_loop(stored, pairs, late, 0)
+        lax.fori_loop(0, (pairs - stored) // 4, late, 0)
 
     push = STIFFNESS * jnp.maximum(-fields[0], 0.0)
     lane = lax.broadcasted_iota(jnp.int32, (pairs, 128), 1)
@@ -304,18 +309,13 @@
     pairs = pair_first.shape[0]
     slots = 8 * capacity
     count = knot_cells.shape[1] // 3
-    stored = min(pairs, 96)
+    stored = min(pairs, 112)
     lists = send_list.reshape(8, capacity)
-    span = max(slots, pairs)
-    rows = jnp.stack([
-        jnp.pad(v, (0, span - v.shape[0]))
-        for v in (lists.reshape(-1), pair_first, pair_sdf, pair_live)
-    ] + [jnp.zeros((span,), jnp.int32)] * 4)
     vmem = pl.BlockSpec(memory_space=pltpu.VMEM)
     return pl.pallas_call(
         functools.partial(kernel, n_row, n_col, stored),
         out_shape=jax.ShapeDtypeStruct((6, grains), F32),
-        in_specs=[vmem] * 7,
+        in_specs=[vmem] * 9,
         out_specs=vmem,
         scratch_shapes=[
             pltpu.VMEM((slots, cells), BF16),
@@ -336,8 +336,9 @@
             pltpu.SemaphoreType.DMA((8,)),
         ],
         compiler_params=pltpu.CompilerParams(
-            collective_id=0, has_side_effects=True, vmem_limit_bytes=60 * 2**20),
-    )(sdf_grids, grain_poses, surface_nodes, lists, rows, knot_cells, offsets)
+            collective_id=0, has_side_effects=True, vmem_limit_bytes=62 * 2**20),
+    )(sdf_grids, grain_poses, surface_nodes, lists, pair_first.reshape(1, pairs),
+      pair_sdf.reshape(1, pairs), pair_live.reshape(1, pairs), knot_cells, offsets)
 
 
 def solution(mesh):

time: 66.9 us -> 55.3 us (0.83)
  Pallas kernels: 61.8 us -> 53.7 us
  local copies, waits for them, and re-layouts: 4.68 us -> 1.32 us
    pallas_call x1, Pallas kernels: 61.8 us -> 53.7 us  [local(): pl.pallas_call(functools.partial(kernel, n_row, n_col, stored), out_shape...]
    pad x3 -> x0, local copies, waits for them, and re-layouts: 1.97 us -> none  [local(): jnp.pad(v, (0, span - v.shape[0]))]
    another operation x3 -> x0, local copies, waits for them, and re-layouts: 1.38 us -> none  [local(): jnp.stack([jnp.pad(v, (0, span - v.shape[0])) for v in (lists.reshape(-1)...]
where the time goes in v2:
time: 55.3 us; the launch traced here: 55.1 us
  Pallas kernels  53.7 us (97%)
  local copies, waits for them, and re-layouts  1.32 us (2%)
    pallas_call x1, Pallas kernels, local(): pl.pallas_call(functools.partial(kernel, n_row, n_col, stored), out_shape...  53.7 us
    unnamed x1, local copies, waits for them, and re-layouts  1.32 us

profile of v2, /device:TPU:0, one launch (start us, length us, event | category | flops | bytes accessed | tf_op | source)
XLA Modules:
  0.0 55.1 jit_solution(7634738712003919258)
XLA Ops:
  0.0 53.7 %shard_map.91 = f32[6,512]{1,0:T(8,128)} custom-call(bf16[512,4096]{1,0:T(8,128)(2,1)} %grids.1, f32[12,512]{1,0:T(8,128)} %poses.1, f32[512,768]{1,0:T(8,128)} %nodes.1, s32[8,32]{1,0:T(8,128)} %bitcast.4, s32[1,128]{1,0:T(1,128)} %bitcast.5, s32[1,128]{1,0:T(1,128)} %bitcast.6, s32[1,128]{1,0:T(1,128)} %bitcast.7, s32[128,768]{1,0:T(8,128)} %knots.1, ...), custom_call_target="tpu_custom_call" | custom-call | tf_op jit(solution)/shard_map/pallas_call | solution.py:315
  53.7 1.3 %copy.11 = f32[6,512]{1,0:T(8,128)} copy(f32[6,512]{1,0:T(8,128)} %shard_map.91) | data formatting | bytes 24576

commit v3 on v2

--- a/solution.py
+++ b/solution.py
@@ -309,7 +309,7 @@
     pairs = pair_first.shape[0]
     slots = 8 * capacity
     count = knot_cells.shape[1] // 3
-    stored = min(pairs, 112)
+    stored = min(pairs, 120)
     lists = send_list.reshape(8, capacity)
     vmem = pl.BlockSpec(memory_space=pltpu.VMEM)
     return pl.pallas_call(
@@ -336,7 +336,7 @@
             pltpu.SemaphoreType.DMA((8,)),
         ],
         compiler_params=pltpu.CompilerParams(
-            collective_id=0, has_side_effects=True, vmem_limit_bytes=62 * 2**20),
+            collective_id=0, has_side_effects=True, vmem_limit_bytes=64 * 2**20 - 65536),
     )(sdf_grids, grain_poses, surface_nodes, lists, pair_first.reshape(1, pairs),
       pair_sdf.reshape(1, pairs), pair_live.reshape(1, pairs), knot_cells, offsets)
 

time: 55.3 us -> 54.8 us (level)
  no operation moved by 1% of the time
where the time goes in v3:
time: 54.8 us; the launch traced here: 54.5 us
  Pallas kernels  53.2 us (97%)
  local copies, waits for them, and re-layouts  1.32 us (2%)
    pallas_call x1, Pallas kernels, local(): pl.pallas_call(functools.partial(kernel, n_row, n_col, stored), out_shape...  53.2 us
    unnamed x1, local copies, waits for them, and re-layouts  1.32 us

profile of v3, /device:TPU:0, one launch (start us, length us, event | category | flops | bytes accessed | tf_op | source)
XLA Modules:
  0.0 54.5 jit_solution(2588058133123525391)
XLA Ops:
  0.0 53.2 %shard_map.91 = f32[6,512]{1,0:T(8,128)} custom-call(bf16[512,4096]{1,0:T(8,128)(2,1)} %grids.1, f32[12,512]{1,0:T(8,128)} %poses.1, f32[512,768]{1,0:T(8,128)} %nodes.1, s32[8,32]{1,0:T(8,128)} %bitcast.4, s32[1,128]{1,0:T(1,128)} %bitcast.5, s32[1,128]{1,0:T(1,128)} %bitcast.6, s32[1,128]{1,0:T(1,128)} %bitcast.7, s32[128,768]{1,0:T(8,128)} %knots.1, ...), custom_call_target="tpu_custom_call" | custom-call | tf_op jit(solution)/shard_map/pallas_call | solution.py:315
  53.2 1.3 %copy.11 = f32[6,512]{1,0:T(8,128)} copy(f32[6,512]{1,0:T(8,128)} %shard_map.91) | data formatting | bytes 24576
